TPU v7x, 32 devices: a whole 2x2x4 slice. The times are simulated.
32 devices in a mesh: tile: 16 (over z, y, x), dp: 2 (over core).
Axes of the slice: x: 2, y: 2, z: 4, core: 2. Of those that a mesh axis runs over, the one named last changes fastest.
Arguments:
- features: bfloat16 [2, 192, 384, 128], P('dp', 'tile'), may hold values from -6 to 6
- cotangent: bfloat16 [2, 192, 384, 128], P('dp', 'tile'), may hold values from -6 to 6
- tile_mask: int32 [2, 16, 32], P('dp', 'tile'), may hold values from 0 to 1, as said below
- work_lists: int32 [2, 16, 22], P('dp'), may hold values from 0 to 511, as said below
- dilations: int32 [2, 16], P('dp'), may hold values from 1 to 2
- conv_weight: bfloat16 [3, 3, 128, 128], replicated, may hold values from -0.1875 to 0.1875
- conv_bias: float32 [128], replicated, may hold values from -4 to 4
Outputs:
- input_grad: bfloat16 [2, 192, 384, 128], P('dp', 'tile')
- weight_grads: float32 [147456], P(('tile', 'dp'))
Inputs may be any that keep to these rules, and one draw needn't show every extreme that they name: `tile_mask`: exactly 352 tiles of each copy are 1. `work_lists`: for each copy, the work lists name every tile whose mask is 1 exactly once, as row * 32 + column, 22 for each worker; at most 2 of one worker's ids lie in one row of tiles, and in every draw some worker has 2 ids in one row.
All inputs are finite; a program needn't handle non-finite values.
Results may differ from a plain program's by a relative error of at most 0.0055.
Values may be sent and summed in bfloat16 or wider, within the bound.
No kernel may reach another device: no remote copies, remote signals or barrier semaphores. Data moves between devices by JAX's collectives and lax.ppermute only.
A program may use at most 128 MiB of HBM per device.

v0:
```python
import functools
import math

import jax
import jax.numpy as jnp
from jax import lax
from jax.experimental import pallas as pl
from jax.experimental.pallas import tpu as pltpu
from jax.sharding import PartitionSpec as P

TILE = 12
HALO = 2
LANES = 128
EDGE = 8
VMEM_LIMIT = 48 * 1024 * 1024

F32 = jnp.float32
BF16 = jnp.bfloat16


def expand_mask(obs_ref, row, columns):
    first = TILE * lax.broadcasted_iota(jnp.int32, (columns, LANES), 1)
    cell = lax.broadcasted_iota(jnp.int32, (columns, LANES), 0)
    inside = (cell >= first) & (cell < first + TILE)
    picked = jnp.where(inside, obs_ref[row : row + 1, :], 0.0).astype(BF16)
    return jnp.dot(picked, jnp.ones((LANES, LANES), BF16), preferred_element_type=F32)


def pair_start(index, rate):
    return jnp.where(rate == 1, 2 * index, 4 * (index // 2) + index % 2)


def shifted_three(pad_ref, rate, sign, columns):
    return [
        pad_ref[pl.ds(EDGE - sign * rate, columns), :].astype(BF16),
        pad_ref[pl.ds(EDGE, columns), :].astype(BF16),
        pad_ref[pl.ds(EDGE + sign * rate, columns), :].astype(BF16),
    ]


def taps_kernel(
    rate_ref, obs_ref, low_ref, x_ref, high_ref, cot_ref, w_ref, bias_ref,
    tap_ref, grad_ref,
    pad, masks, xcat, xt, gcat, wide, total, flat,
):
    columns, channels = x_ref.shape[1], x_ref.shape[2]
    rate = rate_ref[0]
    for row in range(3):
        masks[row] = expand_mask(obs_ref, row, columns)
    pad[:EDGE] = jnp.zeros((EDGE, channels), F32)
    pad[EDGE + columns :] = jnp.zeros((EDGE, channels), F32)
    for row in range(4):
        for out in range(2):
            tap = row - out
            for col in range(3):
                block = (
                    w_ref[tap * 3 + col] if 0 <= tap < 3 else jnp.zeros((channels, channels), BF16)
                )
                start = (row * 3 + col) * channels
                wide[start : start + channels, out * channels : (out + 1) * channels] = block

    def prepare(source, row, target, mask):
        value = source[row].astype(F32) * masks[mask]
        pad[EDGE : EDGE + columns] = value
        left, here, right = shifted_three(pad, rate, 1, columns)
        xcat[target, :, :channels] = left
        xcat[target, :, channels : 2 * channels] = here
        xcat[target, :, 2 * channels :] = right
        xt[target] = here.T

    for row in range(HALO):
        prepare(low_ref, row, row, 0)
        prepare(high_ref, row, HALO + TILE + row, 2)

    @pl.loop(0, TILE)
    def _(row):
        prepare(x_ref, row, HALO + row, 1)

    total[...] = jnp.zeros_like(total)

    @pl.loop(0, TILE // 2)
    def _(index):
        first = pair_start(index, rate)
        rows = jnp.concatenate([xcat[first + HALO + rate * (k - 1)] for k in range(4)], axis=1)
        both = jnp.dot(rows, wide[...], preferred_element_type=F32)
        for out in range(2):
            row = first + rate * out
            pre = both[:, out * channels : (out + 1) * channels] + bias_ref[...]
            sig = 0.5 * jnp.tanh(0.5 * pre) + 0.5
            grad = cot_ref[row].astype(F32) * masks[1] * sig * (1.0 + pre * (1.0 - sig))
            grad_ref[row] = grad.astype(BF16)
            pad[EDGE : EDGE + columns] = grad
            left, here, right = shifted_three(pad, rate, -1, columns)
            part = slice(out * columns, (out + 1) * columns)
            gcat[part, :channels] = left
            gcat[part, channels : 2 * channels] = here
            gcat[part, 2 * channels :] = right
        flipped = jnp.concatenate(
            [
                jnp.concatenate(
                    [xt[first + HALO + rate * (a + out)] for out in range(2)], axis=1
                )
                for a in (-1, 0, 1)
            ],
            axis=0,
        )
        total[...] += jnp.dot(flipped, gcat[...], preferred_element_type=F32)

    for a in range(3):
        for b in range(3):
            start = (a * 3 + b) * channels
            flat[start : start + channels] = total[
                a * channels : (a + 1) * channels, b * channels : (b + 1) * channels
            ]
    share = tap_ref.shape[1]
    for part in range(tap_ref.shape[0]):
        tap_ref[part] = flat[part * share : (part + 1) * share].astype(BF16)


def inputs_kernel(
    rate_ref, obs_ref, grad_ref, cot_ref, w_ref,
    out_ref, edge_ref, low_ref, high_ref,
    pad, mask, gcat, wide, sums,
):
    columns, channels = grad_ref.shape[1], grad_ref.shape[2]
    rate = rate_ref[0]
    mask[...] = expand_mask(obs_ref, 1, columns)
    pad[:EDGE] = jnp.zeros((EDGE, channels), F32)
    pad[EDGE + columns :] = jnp.zeros((EDGE, channels), F32)
    for row in range(4):
        for out in range(2):
            tap = out + 2 - row
            for col in range(3):
                block = (
                    w_ref[tap * 3 + col] if 0 <= tap < 3 else jnp.zeros((channels, channels), BF16)
                )
                start = (row * 3 + col) * channels
                wide[out * channels : (out + 1) * channels, start : start + channels] = block
    rim = jnp.zeros((2 * HALO,) + gcat.shape[1:], BF16)
    gcat[: 2 * HALO] = rim
    gcat[2 * HALO + TILE :] = rim

    @pl.loop(0, TILE)
    def _(row):
        pad[EDGE : EDGE + columns] = grad_ref[row].astype(F32)
        left, here, right = shifted_three(pad, rate, -1, columns)
        gcat[2 * HALO + row, :, :channels] = left
        gcat[2 * HALO + row, :, channels : 2 * channels] = here
        gcat[2 * HALO + row, :, 2 * channels :] = right

    @pl.loop(0, TILE // 2 + HALO)
    def _(index):
        first = pair_start(index, rate)
        rows = jnp.concatenate([gcat[first + HALO + rate * (k - 1)] for k in range(4)], axis=1)
        both = lax.dot_general(
            rows, wide[...], (((1,), (1,)), ((), ())), preferred_element_type=F32
        )
        for out in range(2):
            sums[first + rate * out] = both[:, out * channels : (out + 1) * channels]

    for row in range(HALO):
        low_ref[row] = sums[row].astype(BF16)
        high_ref[row] = sums[HALO + TILE + row].astype(BF16)
        edge_ref[row] = sums[HALO + row] + cot_ref[row].astype(F32)
        edge_ref[HALO + row] = sums[TILE + row] + cot_ref[TILE - HALO + row].astype(F32)
    for row in range(HALO, TILE - HALO):
        value = (sums[HALO + row] + cot_ref[row].astype(F32)) * mask[...]
        out_ref[row] = value.astype(BF16)


def edges_kernel(obs_ref, edge_ref, rim_ref, held_ref, out_ref):
    del held_ref
    mask = expand_mask(obs_ref, 1, edge_ref.shape[1])
    for row in range(HALO):
        value = (edge_ref[row] + rim_ref[row].astype(F32)) * mask
        out_ref[row] = value.astype(BF16)


def exchange(to_next, to_previous, axis):
    count = lax.axis_size(axis)
    forward = [(i, i + 1) for i in range(count - 1)]
    backward = [(target, source) for source, target in forward]
    return lax.ppermute(to_next, axis, forward), lax.ppermute(to_previous, axis, backward)


def shards(features, cotangent, tile_mask, work_lists, dilations, conv_weight, conv_bias):
    x, cot = features[0], cotangent[0]
    columns, channels = x.shape[1], x.shape[2]
    tiles_row = columns // TILE
    axes = ("tile", "dp")
    devices = lax.axis_size("tile") * lax.axis_size("dp")
    my_index = lax.axis_index("tile")

    low, high = exchange(x[TILE - HALO :], x[:HALO], "tile")

    rate = lax.dynamic_slice_in_dim(dilations[0], my_index, 1)
    row_ids = my_index - 1 + jnp.arange(8, dtype=jnp.int32)
    lane = jnp.arange(LANES, dtype=jnp.int32)
    targets = jnp.where(lane < tiles_row, row_ids[:, None] * tiles_row + lane, -1)
    ids = work_lists[0].reshape(-1)
    observed = jnp.any(ids[:, None, None] == targets[None], axis=0).astype(F32)
    weight = conv_weight.reshape(9, channels, channels)
    bias = conv_bias.reshape(1, channels)

    smem = pl.BlockSpec(memory_space=pltpu.SMEM)
    vmem = pl.BlockSpec(memory_space=pltpu.VMEM)
    params = pltpu.CompilerParams(vmem_limit_bytes=VMEM_LIMIT)
    rows_total = 9 * channels
    direct = rows_total % devices == 0
    shape_taps = (devices, rows_total // devices) if direct else (1, rows_total)

    taps, grad = pl.pallas_call(
        taps_kernel,
        out_shape=(
            jax.ShapeDtypeStruct(shape_taps + (channels,), BF16),
            jax.ShapeDtypeStruct((TILE, columns, channels), BF16),
        ),
        in_specs=[smem] + [vmem] * 7,
        out_specs=(vmem, vmem),
        scratch_shapes=[
            pltpu.VMEM((columns + 2 * EDGE, channels), F32),
            pltpu.VMEM((3, columns, channels), F32),
            pltpu.VMEM((TILE + 2 * HALO, columns, 3 * channels), BF16),
            pltpu.VMEM((TILE + 2 * HALO, channels, columns), BF16),
            pltpu.VMEM((2 * columns, 3 * channels), BF16),
            pltpu.VMEM((12 * channels, 2 * channels), BF16),
            pltpu.VMEM((3 * channels, 3 * channels), F32),
            pltpu.VMEM((rows_total, channels), F32),
        ],
        compiler_params=params,
        name="taps",
    )(rate, observed, low, x, high, cot, weight, bias)

    if not direct:
        taps = taps.reshape(devices, -1)
    received = lax.all_to_all(taps, axes, 0, 0, tiled=True)

    held, edge, to_low, to_high = pl.pallas_call(
        inputs_kernel,
        out_shape=(
            jax.ShapeDtypeStruct((TILE, columns, channels), BF16),
            jax.ShapeDtypeStruct((2 * HALO, columns, channels), F32),
            jax.ShapeDtypeStruct((HALO, columns, channels), BF16),
            jax.ShapeDtypeStruct((HALO, columns, channels), BF16),
        ),
        in_specs=[smem] + [vmem] * 4,
        out_specs=(vmem,) * 4,
        scratch_shapes=[
            pltpu.VMEM((columns + 2 * EDGE, channels), F32),
            pltpu.VMEM((columns, channels), F32),
            pltpu.VMEM((TILE + 4 * HALO, columns, 3 * channels), BF16),
            pltpu.VMEM((2 * channels, 12 * channels), BF16),
            pltpu.VMEM((TILE + 2 * HALO, columns, channels), F32),
        ],
        compiler_params=params,
        name="inputs",
    )(rate, observed, grad, cot, weight)

    from_low, from_high = exchange(to_high, to_low, "tile")
    rims = jnp.concatenate([from_low, from_high], axis=0)
    block = (HALO, columns, channels)
    last = TILE // HALO - 1
    input_grad = pl.pallas_call(
        edges_kernel,
        grid=(2,),
        out_shape=jax.ShapeDtypeStruct((TILE, columns, channels), BF16),
        in_specs=[
            pl.BlockSpec((8, LANES), lambda i: (0, 0)),
            pl.BlockSpec(block, lambda i: (i, 0, 0)),
            pl.BlockSpec(block, lambda i: (i, 0, 0)),
            pl.BlockSpec(memory_space=pl.ANY),
        ],
        out_specs=pl.BlockSpec(block, lambda i: (i * last, 0, 0)),
        input_output_aliases={3: 0},
        compiler_params=params,
        name="edges",
    )(observed, edge, rims, held)

    grad_scale = 1.0 / math.sqrt(devices * work_lists.shape[2] * TILE * TILE)
    summed = jnp.sum(received.astype(F32), axis=0) * grad_scale
    return (input_grad[None], summed.reshape(-1))


def solution(mesh):
    placed = (
        P("dp", "tile", None, None),
        P("dp", "tile", None, None),
        P("dp", "tile", None),
        P("dp", None, None),
        P("dp", None),
        P(),
        P(),
    )
    return jax.shard_map(
        shards,
        mesh=mesh,
        in_specs=placed,
        out_specs=(P("dp", "tile", None, None), P(("tile", "dp"))),
        check_vma=False,
    )
```

profile of v0, /device:TPU:0, one launch (start us, length us, event | category | flops | bytes accessed | tf_op | source)
XLA Modules:
  0.0 61.9 jit_solution(11961612354987794712)
XLA Ops:
  0.6 0.0 copy-start
  0.6 1.1 %slice_bitcast_fusion = (bf16[2,384,128]{2,1,0:T(8,128)(2,1)S(1)}, bf16[2,384,128]{2,1,0:T(8,128)(2,1)S(1)}) fusion(bf16[1,12,384,128]{3,2,1,0:T(8,128)(2,1)} %param.7), kind=kLoop, calls=%fused_computation.3 | loop fusion | bytes 786432 | tf_op jit(solution)/shard_map/slice | solution.py:194
  1.7 1.3 %collective-permute-start.1 = (bf16[2,384,128]{2,1,0:T(8,128)(2,1)S(1)}, bf16[2,384,128]{2,1,0:T(8,128)(2,1)S(1)}, u32[]{:S(2)}, u32[]{:S(2)}) collective-permute-start(bf16[2,384,128]{2,1,0:T(8,128)(2,1)S(1)} %get-tuple-element.14), channel_id=1, source_target_pairs={{2,0},{4,2},{6,4},{8,6},{10,8},{12,10},{14,12},{16,14},{18,16},{20... | collective-permute-start | bytes 589832 | tf_op jit(solution)/shard_map/ppermute | solution.py:183
  3.0 5.5 %collective-permute-start = (bf16[2,384,128]{2,1,0:T(8,128)(2,1)S(1)}, bf16[2,384,128]{2,1,0:T(8,128)(2,1)S(1)}, u32[]{:S(2)}, u32[]{:S(2)}) collective-permute-start(bf16[2,384,128]{2,1,0:T(8,128)(2,1)S(1)} %get-tuple-element.15), channel_id=1, source_target_pairs={{0,2},{2,4},{4,6},{6,8},{8,10},{10,12},{12,14},{14,16},{16,18},{18... | collective-permute-start | bytes 589832 | tf_op jit(solution)/shard_map/ppermute | solution.py:183
  8.5 0.1 add_select_fusion
  8.6 0.8 %eq.15 = s32[352]{0:T(512)S(1)} reshape(s32[1,16,22]{2,1,0:T(8,128)} %param.9) | data formatting | bytes 2816 | tf_op jit(solution)/shard_map/eq | solution.py:201
  9.4 1.1 %compare_reduce_fusion = pred[8,128]{1,0:T(8,128)(4,1)S(1)} fusion(s32[8,128]{1,0:T(8,128)S(1)} %add_select_fusion, s32[352]{0:T(512)S(1)} %eq.15), kind=kLoop, calls=%fused_computation | loop fusion | flops 719872 | bytes 6528 | tf_op jit(solution)/shard_map/reduce_or | solution.py:201
  10.5 0.0 copy-done
  10.5 0.6 constant_dynamic-slice_fusion
  11.1 0.4 collective-permute-done.1.high_ref
  11.4 5.3 %collective-permute-done.low_ref = bf16[2,384,128]{2,1,0:T(8,128)(2,1)S(1)} collective-permute-done((bf16[2,384,128]{2,1,0:T(8,128)(2,1)S(1)}, bf16[2,384,128]{2,1,0:T(8,128)(2,1)S(1)}, u32[]{:S(2)}, u32[]{:S(2)}) %collective-permute-start) | collective-permute-done | bytes 196640 | tf_op jit(solution)/shard_map/ppermute | solution.py:183
  16.8 0.0 copy-start.1
  16.8 1.3 %copy-done.1 = bf16[1,12,384,128]{3,2,1,0:T(8,128)(2,1)S(1)} copy-done((bf16[1,12,384,128]{3,2,1,0:T(8,128)(2,1)S(1)}, bf16[1,12,384,128]{3,2,1,0:T(8,128)(2,1)}, u32[]{:S(2)}) %copy-start.1) | copy-done | bytes 1179672
  18.0 0.0 copy-start.3
  18.0 1.3 %copy-done.3 = bf16[1,12,384,128]{3,2,1,0:T(8,128)(2,1)S(1)} copy-done((bf16[1,12,384,128]{3,2,1,0:T(8,128)(2,1)S(1)}, bf16[1,12,384,128]{3,2,1,0:T(8,128)(2,1)}, u32[]{:S(2)}) %copy-start.3) | copy-done | bytes 1179672
  19.3 0.0 copy-start.4
  19.3 1.0 %copy-done.4 = bf16[3,3,128,128]{3,2,1,0:T(8,128)(2,1)S(1)} copy-done((bf16[3,3,128,128]{3,2,1,0:T(8,128)(2,1)S(1)}, bf16[3,3,128,128]{3,2,1,0:T(8,128)(2,1)}, u32[]{:S(2)}) %copy-start.4) | copy-done | bytes 294936
  20.3 0.0 copy-start.6
  20.3 0.7 %copy-done.6 = f32[128]{0:T(128)S(1)} copy-done((f32[128]{0:T(128)S(1)}, f32[128]{0:T(128)}, u32[]{:S(2)}) %copy-start.6) | copy-done | bytes 536
  20.9 12.9 %taps.1 = (bf16[32,36,128]{2,1,0:T(8,128)(2,1)}, bf16[12,384,128]{2,1,0:T(8,128)(2,1)S(1)}) custom-call(s32[1]{0:T(128)} %bitcast.rate_ref, f32[8,128]{1,0:T(8,128)S(1)} %convert_element_type.6.obs_ref, bf16[2,384,128]{2,1,0:T(8,128)(2,1)S(1)} %collective-permute-done.low_ref, bf16[12,384,128]{2,1,0:T(8,128)(2,1)S(1)} %bitcast.14, ...), custom_call_target="tpu_custom_call" | custom-call | tf_op jit(solution)/shard_map/taps/pallas_call | solution.py:212
  33.9 4.9 %all-to-all-start = ((bf16[32,36,128]{2,1,0:T(8,128)(2,1)}), bf16[32,36,128]{2,1,0:T(8,128)(2,1)S(1)}, u32[]{:S(2)}, u32[]{:S(2)}) async-start(bf16[32,36,128]{2,1,0:T(8,128)(2,1)} %get-tuple-element.13), calls=%async_computation | async-start | bytes 655360 | tf_op jit(solution)/shard_map/all_to_all | solution.py:236
  38.8 0.0 copy-done.2
  38.8 0.0 copy-done.5
  38.8 7.1 %inputs.1 = (bf16[12,384,128]{2,1,0:T(8,128)(2,1)}, f32[4,384,128]{2,1,0:T(8,128)S(1)}, bf16[2,384,128]{2,1,0:T(8,128)(2,1)S(1)}, bf16[2,384,128]{2,1,0:T(8,128)(2,1)S(1)}) custom-call(s32[1]{0:T(128)} %bitcast.rate_ref, f32[8,128]{1,0:T(8,128)S(1)} %convert_element_type.6.obs_ref, bf16[12,384,128]{2,1,0:T(8,128)(2,1)S(1)} %get-tuple-element.8.grad_ref, ...), custom_call_target="tpu_custom_call" | custom-call | tf_op jit(solution)/shard_map/inputs/pallas_call | solution.py:238
  45.9 3.6 %collective-permute-start.2 = (bf16[2,384,128]{2,1,0:T(8,128)(2,1)S(1)}, bf16[2,384,128]{2,1,0:T(8,128)(2,1)S(1)}, u32[]{:S(2)}, u32[]{:S(2)}) collective-permute-start(bf16[2,384,128]{2,1,0:T(8,128)(2,1)S(1)} %get-tuple-element.10), channel_id=1, source_target_pairs={{0,2},{2,4},{4,6},{6,8},{8,10},{10,12},{12,14},{14,16},{16,18},{18... | collective-permute-start | bytes 589832 | tf_op jit(solution)/shard_map/ppermute | solution.py:183
  49.5 1.3 %collective-permute-start.3 = (bf16[2,384,128]{2,1,0:T(8,128)(2,1)S(1)}, bf16[2,384,128]{2,1,0:T(8,128)(2,1)S(1)}, u32[]{:S(2)}, u32[]{:S(2)}) collective-permute-start(bf16[2,384,128]{2,1,0:T(8,128)(2,1)S(1)} %get-tuple-element.11), channel_id=1, source_target_pairs={{2,0},{4,2},{6,4},{8,6},{10,8},{12,10},{14,12},{16,14},{18,16},{20... | collective-permute-start | bytes 589832 | tf_op jit(solution)/shard_map/ppermute | solution.py:183
  50.8 3.2 %collective-permute-done.2 = bf16[2,384,128]{2,1,0:T(8,128)(2,1)S(1)} collective-permute-done((bf16[2,384,128]{2,1,0:T(8,128)(2,1)S(1)}, bf16[2,384,128]{2,1,0:T(8,128)(2,1)S(1)}, u32[]{:S(2)}, u32[]{:S(2)}) %collective-permute-start.2) | collective-permute-done | bytes 196640 | tf_op jit(solution)/shard_map/ppermute | solution.py:183
  54.0 6.1 %collective-permute-done.3 = bf16[2,384,128]{2,1,0:T(8,128)(2,1)S(1)} collective-permute-done((bf16[2,384,128]{2,1,0:T(8,128)(2,1)S(1)}, bf16[2,384,128]{2,1,0:T(8,128)(2,1)S(1)}, u32[]{:S(2)}, u32[]{:S(2)}) %collective-permute-start.3) | collective-permute-done | bytes 196640 | tf_op jit(solution)/shard_map/ppermute | solution.py:183
  60.2 1.1 %edges.1 = bf16[12,384,128]{2,1,0:T(8,128)(2,1)} custom-call(f32[8,128]{1,0:T(8,128)S(1)} %convert_element_type.6.obs_ref, f32[4,384,128]{2,1,0:T(8,128)S(1)} %get-tuple-element.9.edge_ref, bf16[4,384,128]{2,1,0:T(8,128)(2,1)S(1)} %pad_maximum_fusion.rim_ref, bf16[12,384,128]{2,1,0:T(8,128)(2,1)} %get-tuple-element.12.held_ref), custom_call_target="tpu_custom_call", output_to_operand_aliasing={{}: (3, {})} | custom-call | tf_op jit(solution)/shard_map/edges/pallas_call | solution.py:263
  61.2 0.0 all-to-all-done
  61.2 0.1 convert_reduce_fusion
  61.3 0.6 multiply_bitcast_fusion
  (6 shorter events, 0.1 us)
Async XLA Ops:
  0.6 9.9 %copy-start = (s32[1,16]{1,0:T(1,128)S(1)}, s32[1,16]{1,0:T(1,128)}, u32[]{:S(2)}) copy-start(s32[1,16]{1,0:T(1,128)} %param.10) | copy-start | bytes 196
  1.7 9.7 %collective-permute-start.1 = (bf16[2,384,128]{2,1,0:T(8,128)(2,1)S(1)}, bf16[2,384,128]{2,1,0:T(8,128)(2,1)S(1)}, u32[]{:S(2)}, u32[]{:S(2)}) collective-permute-start(bf16[2,384,128]{2,1,0:T(8,128)(2,1)S(1)} %get-tuple-element.14), channel_id=1, source_target_pairs={{2,0},{4,2},{6,4},{8,6},{10,8},{12,10},{14,12},{16,14},{18,16},{20... | collective-permute-start | bytes 589832 | tf_op jit(solution)/shard_map/ppermute | solution.py:183
  3.0 13.8 %collective-permute-start = (bf16[2,384,128]{2,1,0:T(8,128)(2,1)S(1)}, bf16[2,384,128]{2,1,0:T(8,128)(2,1)S(1)}, u32[]{:S(2)}, u32[]{:S(2)}) collective-permute-start(bf16[2,384,128]{2,1,0:T(8,128)(2,1)S(1)} %get-tuple-element.15), channel_id=1, source_target_pairs={{0,2},{2,4},{4,6},{6,8},{8,10},{10,12},{12,14},{14,16},{16,18},{18... | collective-permute-start | bytes 589832 | tf_op jit(solution)/shard_map/ppermute | solution.py:183
  16.8 1.3 %copy-start.1 = (bf16[1,12,384,128]{3,2,1,0:T(8,128)(2,1)S(1)}, bf16[1,12,384,128]{3,2,1,0:T(8,128)(2,1)}, u32[]{:S(2)}) copy-start(bf16[1,12,384,128]{3,2,1,0:T(8,128)(2,1)} %param.8) | copy-start | bytes 3538948
  18.0 1.3 %copy-start.3 = (bf16[1,12,384,128]{3,2,1,0:T(8,128)(2,1)S(1)}, bf16[1,12,384,128]{3,2,1,0:T(8,128)(2,1)}, u32[]{:S(2)}) copy-start(bf16[1,12,384,128]{3,2,1,0:T(8,128)(2,1)} %param.7) | copy-start | bytes 3538948
  19.3 1.0 %copy-start.4 = (bf16[3,3,128,128]{3,2,1,0:T(8,128)(2,1)S(1)}, bf16[3,3,128,128]{3,2,1,0:T(8,128)(2,1)}, u32[]{:S(2)}) copy-start(bf16[3,3,128,128]{3,2,1,0:T(8,128)(2,1)} %param.11) | copy-start | bytes 884740
  20.3 0.7 %copy-start.6 = (f32[128]{0:T(128)S(1)}, f32[128]{0:T(128)}, u32[]{:S(2)}) copy-start(f32[128]{0:T(128)} %param.12) | copy-start | bytes 1540
  20.9 17.9 %copy-start.2 = (bf16[1,12,384,128]{3,2,1,0:T(8,128)(2,1)S(1)}, bf16[1,12,384,128]{3,2,1,0:T(8,128)(2,1)}, u32[]{:S(2)}) copy-start(bf16[1,12,384,128]{3,2,1,0:T(8,128)(2,1)} %param.8) | copy-start | bytes 3538948
  20.9 17.9 %copy-start.5 = (bf16[3,3,128,128]{3,2,1,0:T(8,128)(2,1)S(1)}, bf16[3,3,128,128]{3,2,1,0:T(8,128)(2,1)}, u32[]{:S(2)}) copy-start(bf16[3,3,128,128]{3,2,1,0:T(8,128)(2,1)} %param.11) | copy-start | bytes 884740
  33.9 27.4 %all-to-all-start = ((bf16[32,36,128]{2,1,0:T(8,128)(2,1)}), bf16[32,36,128]{2,1,0:T(8,128)(2,1)S(1)}, u32[]{:S(2)}, u32[]{:S(2)}) async-start(bf16[32,36,128]{2,1,0:T(8,128)(2,1)} %get-tuple-element.13), calls=%async_computation | async-start | bytes 655360 | tf_op jit(solution)/shard_map/all_to_all | solution.py:236
  45.9 8.1 %collective-permute-start.2 = (bf16[2,384,128]{2,1,0:T(8,128)(2,1)S(1)}, bf16[2,384,128]{2,1,0:T(8,128)(2,1)S(1)}, u32[]{:S(2)}, u32[]{:S(2)}) collective-permute-start(bf16[2,384,128]{2,1,0:T(8,128)(2,1)S(1)} %get-tuple-element.10), channel_id=1, source_target_pairs={{0,2},{2,4},{4,6},{6,8},{8,10},{10,12},{12,14},{14,16},{16,18},{18... | collective-permute-start | bytes 589832 | tf_op jit(solution)/shard_map/ppermute | solution.py:183
  49.5 10.6 %collective-permute-start.3 = (bf16[2,384,128]{2,1,0:T(8,128)(2,1)S(1)}, bf16[2,384,128]{2,1,0:T(8,128)(2,1)S(1)}, u32[]{:S(2)}, u32[]{:S(2)}) collective-permute-start(bf16[2,384,128]{2,1,0:T(8,128)(2,1)S(1)} %get-tuple-element.11), channel_id=1, source_target_pairs={{2,0},{4,2},{6,4},{8,6},{10,8},{12,10},{14,12},{16,14},{18,16},{20... | collective-permute-start | bytes 589832 | tf_op jit(solution)/shard_map/ppermute | solution.py:183
where the time goes:
time: 62.4 us; the launch traced here: 61.9 us
  Pallas kernels  21.1 us (34%)
  starting transfers between devices  16.6 us (27%)
  waiting for transfers between devices  15 us (24%)
  local copies, waits for them, and re-layouts  6.59 us (11%)
  other arithmetic  1.89 us (3%)
  between operations  0.75 us (1%)
    pallas_call x1, Pallas kernels, shards(): pl.pallas_call(taps_kernel, out_shape=(jax.ShapeDtypeStruct(shape_taps +...  12.9 us
    ppermute x2, starting transfers between devices, exchange(): lax.ppermute(to_next, axis, forward)  9.12 us
    ppermute x2, waiting for transfers between devices, exchange(): lax.ppermute(to_next, axis, forward)  8.48 us
    pallas_call x1, Pallas kernels, shards(): pl.pallas_call(inputs_kernel, out_shape=(jax.ShapeDtypeStruct((TILE, colu...  7.07 us
    ppermute x2, waiting for transfers between devices, exchange(): lax.ppermute(to_previous, axis, backward)  6.51 us
    all_to_all x1, starting transfers between devices, shards(): received = lax.all_to_all(taps, axes, 0, 0, tiled=True)  4.93 us
    unnamed x14, local copies, waits for them, and re-layouts  4.17 us
    ppermute x2, starting transfers between devices, exchange(): lax.ppermute(to_previous, axis, backward)  2.58 us
  transfers between devices with their start and end apart: 5, of which 4 were waited for; matrix products, arithmetic and copies ran while one was open for 4% of the time, Pallas kernels for 13%

commit v1 on v0

v1 whole, which is shorter than its diff:
```python
import math

import jax
import jax.numpy as jnp
from jax import lax
from jax.experimental import pallas as pl
from jax.experimental.pallas import tpu as pltpu
from jax.sharding import PartitionSpec as P

TILE = 12
HALO = 2
LANES = 128
EDGE = 8
VMEM_LIMIT = 32 * 1024 * 1024

F32 = jnp.float32
BF16 = jnp.bfloat16


def cell_mask(lists_ref, row, tiles_row, columns):
    ids = lists_ref[...]
    workers, width = ids.shape
    tile = lax.broadcasted_iota(jnp.int32, (tiles_row, width), 0)
    target = row * tiles_row + tile
    found = ids[0:1] == target
    for worker in range(1, workers):
        found = found | (ids[worker : worker + 1] == target)
    named = jnp.dot(
        jnp.where(found, 1.0, 0.0).astype(BF16),
        jnp.ones((width, LANES), BF16),
        preferred_element_type=F32,
    )
    first = TILE * lax.broadcasted_iota(jnp.int32, (columns, tiles_row), 1)
    cell = lax.broadcasted_iota(jnp.int32, (columns, tiles_row), 0)
    inside = (cell >= first) & (cell < first + TILE)
    return jnp.dot(
        jnp.where(inside, 1.0, 0.0).astype(BF16), named.astype(BF16), preferred_element_type=F32
    )


def pair_start(index, rate):
    return jnp.where(rate == 1, 2 * index, 4 * (index // 2) + index % 2)


def clear_ends(pad_ref, columns):
    ends = jnp.zeros((EDGE, pad_ref.shape[-1]), F32)
    pad_ref[:EDGE] = ends
    pad_ref[EDGE + columns :] = ends


def spread(value, pad_ref, target_ref, rate, sign):
    columns, channels = value.shape
    pad_ref[EDGE : EDGE + columns] = value
    target_ref[:, :channels] = pad_ref[pl.ds(EDGE - sign * rate, columns), :].astype(BF16)
    target_ref[:, channels : 2 * channels] = value.astype(BF16)
    target_ref[:, 2 * channels :] = pad_ref[pl.ds(EDGE + sign * rate, columns), :].astype(BF16)


def silu_grad(cot, pre):
    sig = 0.5 * jnp.tanh(0.5 * pre) + 0.5
    return cot * sig * (1.0 + pre * (1.0 - sig))


def add_tap_sums(total_ref, gcat, flipped):
    total_ref[...] += jnp.dot(flipped, gcat, preferred_element_type=F32)


def first_kernel(
    rates_ref, lists_ref, x_hbm, cot_hbm, w_hbm, bias_ref,
    pre_ref, grad_ref, xt_ref, total_ref, mask_ref, cot_ref,
    xbuf, cbuf, wbuf, pad, masks, xcat, gcat, wide, held, sems,
):
    rows, columns, channels = x_hbm.shape
    tiles_row = columns // TILE
    mine = lax.axis_index("tile")
    rate = rates_ref[0, mine]
    step = rows // 3
    loads = [
        pltpu.make_async_copy(
            x_hbm.at[pl.ds(k * step, step)], xbuf.at[pl.ds(k * step, step)], sems.at[k]
        )
        for k in range(3)
    ]
    loads.append(pltpu.make_async_copy(w_hbm, wbuf, sems.at[3]))
    loads.append(pltpu.make_async_copy(cot_hbm, cbuf, sems.at[4]))
    for load in loads:
        load.start()
    for k in range(3):
        value = cell_mask(lists_ref, mine + k - 1, tiles_row, columns)
        masks[k] = value
        mask_ref[k] = value.astype(BF16)
    clear_ends(pad, columns)
    none = jnp.zeros((HALO,) + xcat.shape[1:], BF16)
    xcat[:HALO] = none
    xcat[HALO + rows :] = none

    for k in range(3):
        loads[k].wait()

        @pl.loop(k * step, (k + 1) * step)
        def _(row):
            value = xbuf[row].astype(F32) * masks[1]
            spread(value, pad, xcat.at[HALO + row], rate, 1)
            xt_ref[row] = value.astype(BF16).T

    loads[3].wait()
    for row in range(4):
        for out in range(2):
            tap = row - out
            for col in range(3):
                block = (
                    wbuf[tap * 3 + col] if 0 <= tap < 3 else jnp.zeros((channels, channels), BF16)
                )
                start = (row * 3 + col) * channels
                wide[start : start + channels, out * channels : (out + 1) * channels] = block

    @pl.loop(0, rows // 2)
    def _(index):
        first = pair_start(index, rate)
        lhs = jnp.concatenate([xcat[first + HALO + rate * (k - 1)] for k in range(4)], axis=1)
        both = jnp.dot(lhs, wide[...], preferred_element_type=F32)
        for out in range(2):
            held[first + rate * out] = (
                both[:, out * channels : (out + 1) * channels] + bias_ref[...]
            )

    loads[4].wait()
    for k in range(HALO):
        for here, row in ((k, k), (HALO + k, rows - HALO + k)):
            pre_ref[here] = held[row]
            cot_ref[here] = (cbuf[row].astype(F32) * masks[1]).astype(BF16)
    total_ref[...] = jnp.zeros_like(total_ref)

    @pl.loop(0, rows // 2 - HALO)
    def _(index):
        first = HALO + 2 * index
        for out in range(2):
            row = first + out
            grad = silu_grad(cbuf[row].astype(F32) * masks[1], held[row])
            grad_ref[row - HALO] = grad.astype(BF16)
            spread(grad, pad, gcat.at[pl.ds(out * columns, columns)], rate, -1)
        flipped = jnp.concatenate(
            [
                jnp.concatenate([xt_ref[first + rate * a + out] for out in range(2)], axis=1)
                for a in (-1, 0, 1)
            ],
            axis=0,
        )
        add_tap_sums(total_ref, gcat[...], flipped)


def rims_kernel(
    rates_ref, low_ref, high_ref, pre_ref, cot_ref, mask_ref, w_ref,
    grad_low_ref, grad_high_ref, xt_ref,
    pad, xcat, terms,
):
    _, columns, channels = low_ref.shape
    rate = rates_ref[0, lax.axis_index("tile")]
    clear_ends(pad, columns)
    for side, ref in enumerate((low_ref, high_ref)):
        mask = mask_ref[2 * side].astype(F32)
        for k in range(HALO):
            value = ref[k].astype(F32) * mask
            spread(value, pad, xcat.at[pl.ds(k * columns, columns)], rate, 1)
            xt_ref[side * HALO + k] = value.astype(BF16).T
        taps = jnp.concatenate([w_ref[6 * side + b] for b in range(3)], axis=0)
        result = jnp.dot(xcat[...], taps, preferred_element_type=F32)
        for k in range(HALO):
            terms[side * HALO + k] = result[k * columns : (k + 1) * columns]
    near = rate == 1
    none = jnp.zeros((columns, channels), F32)
    adds = [
        jnp.where(near, terms[1], terms[0]),
        jnp.where(near, none, terms[1]),
        jnp.where(near, none, terms[2]),
        jnp.where(near, terms[2], terms[3]),
    ]
    for k in range(2 * HALO):
        grad = silu_grad(cot_ref[k].astype(F32), pre_ref[k] + adds[k])
        target = grad_low_ref if k < HALO else grad_high_ref
        target[k % HALO] = grad.astype(BF16)


def taps_kernel(
    rates_ref, grad_low_ref, grad_high_ref, xt_own_ref, xt_halo_ref, total_in_ref,
    tap_ref,
    pad, gcat, xt, total, flat,
):
    _, columns, channels = grad_low_ref.shape
    rows = xt_own_ref.shape[0]
    rate = rates_ref[0, lax.axis_index("tile")]
    clear_ends(pad, columns)
    half = 3 * HALO
    xt[:HALO] = xt_halo_ref[:HALO]
    xt[HALO:half] = xt_own_ref[: 2 * HALO]
    xt[half : half + 2 * HALO] = xt_own_ref[rows - 2 * HALO :]
    xt[half + 2 * HALO :] = xt_halo_ref[HALO:]
    total[...] = total_in_ref[...]
    for side, ref in enumerate((grad_low_ref, grad_high_ref)):
        for k in range(HALO):
            spread(ref[k].astype(F32), pad, gcat.at[pl.ds(k * columns, columns)], rate, -1)
        base = HALO + half * side
        flipped = jnp.concatenate(
            [
                jnp.concatenate([xt[base + rate * a + k] for k in range(HALO)], axis=1)
                for a in (-1, 0, 1)
            ],
            axis=0,
        )
        add_tap_sums(total, gcat[...], flipped)
    for a in range(3):
        for b in range(3):
            start = (a * 3 + b) * channels
            flat[start : start + channels] = total[
                a * channels : (a + 1) * channels, b * channels : (b + 1) * channels
            ]
    share = tap_ref.shape[1]
    for part in range(tap_ref.shape[0]):
        tap_ref[part] = flat[part * share : (part + 1) * share].astype(BF16)


def inputs_kernel(
    rates_ref, grad_ref, grad_low_ref, grad_high_ref, cot_hbm, mask_ref, w_ref,
    out_hbm, edge_ref,
    cbuf, obuf, pad, gcat, wide, sums, sems,
):
    rows, columns, channels = cot_hbm.shape
    rate = rates_ref[0, lax.axis_index("tile")]
    load = pltpu.make_async_copy(cot_hbm, cbuf, sems.at[0])
    load.start()
    clear_ends(pad, columns)
    for row in range(4):
        for out in range(2):
            tap = out + 2 - row
            for col in range(3):
                block = (
                    w_ref[tap * 3 + col] if 0 <= tap < 3 else jnp.zeros((channels, channels), BF16)
                )
                start = (row * 3 + col) * channels
                wide[out * channels : (out + 1) * channels, start : start + channels] = block
    none = jnp.zeros((HALO,) + gcat.shape[1:], BF16)
    gcat[:HALO] = none
    gcat[HALO + rows :] = none
    for k in range(HALO):
        spread(grad_low_ref[k].astype(F32), pad, gcat.at[HALO + k], rate, -1)
        spread(grad_high_ref[k].astype(F32), pad, gcat.at[rows + k], rate, -1)

    @pl.loop(0, rows - 2 * HALO)
    def _(row):
        spread(grad_ref[row].astype(F32), pad, gcat.at[2 * HALO + row], rate, -1)

    @pl.loop(0, rows // 2)
    def _(index):
        first = pair_start(index, rate)
        lhs = jnp.concatenate([gcat[first + HALO + rate * (k - 1)] for k in range(4)], axis=1)
        both = lax.dot_general(
            lhs, wide[...], (((1,), (1,)), ((), ())), preferred_element_type=F32
        )
        for out in range(2):
            sums[first + rate * out] = both[:, out * channels : (out + 1) * channels]

    load.wait()
    inner = rows - 2 * HALO
    for row in range(HALO, rows - HALO):
        value = (sums[row] + cbuf[row].astype(F32)) * mask_ref[1].astype(F32)
        obuf[row - HALO] = value.astype(BF16)
    store = pltpu.make_async_copy(obuf, out_hbm.at[pl.ds(HALO, inner)], sems.at[1])
    store.start()
    for k in range(HALO):
        for here, row in ((k, k), (HALO + k, rows - HALO + k)):
            edge_ref[here] = sums[row] + cbuf[row].astype(F32)
    store.wait()


def edges_kernel(
    rates_ref, low_ref, high_ref, edge_ref, mask_ref, w_ref, held_hbm,
    out_hbm,
    obuf, pad, gcat, terms, sems,
):
    del held_hbm
    _, columns, channels = low_ref.shape
    rows = out_hbm.shape[0]
    mine = lax.axis_index("tile")
    last = rates_ref.shape[1] - 1
    rates = (rates_ref[0, jnp.maximum(mine - 1, 0)], rates_ref[0, jnp.minimum(mine + 1, last)])
    clear_ends(pad, columns)
    for side, ref in enumerate((low_ref, high_ref)):
        for k in range(HALO):
            spread(
                ref[k].astype(F32), pad, gcat.at[pl.ds(k * columns, columns)], rates[side], -1
            )
        taps = jnp.concatenate([w_ref[6 * (1 - side) + b] for b in range(3)], axis=1)
        result = lax.dot_general(
            gcat[...], taps, (((1,), (1,)), ((), ())), preferred_element_type=F32
        )
        for k in range(HALO):
            terms[side * HALO + k] = result[k * columns : (k + 1) * columns]
    none = jnp.zeros((columns, channels), F32)
    adds = [
        jnp.where(rates[0] == 1, terms[1], terms[0]),
        jnp.where(rates[0] == 1, none, terms[1]),
        jnp.where(rates[1] == 1, none, terms[2]),
        jnp.where(rates[1] == 1, terms[2], terms[3]),
    ]
    for k in range(2 * HALO):
        obuf[k] = ((edge_ref[k] + adds[k]) * mask_ref[1].astype(F32)).astype(BF16)
    stores = [
        pltpu.make_async_copy(
            obuf.at[pl.ds(HALO * side, HALO)],
            out_hbm.at[pl.ds((rows - HALO) * side, HALO)],
            sems.at[side],
        )
        for side in range(2)
    ]
    for store in stores:
        store.start()
    for store in stores:
        store.wait()


def exchange(to_next, to_previous, axis):
    count = lax.axis_size(axis)
    forward = [(i, i + 1) for i in range(count - 1)]
    backward = [(target, source) for source, target in forward]
    return lax.ppermute(to_next, axis, forward), lax.ppermute(to_previous, axis, backward)


def call(kernel, name, outs, specs, scratch, cost, aliases=None):
    memory = {"s": pltpu.SMEM, "v": pltpu.VMEM, "h": pltpu.HBM}
    ins, results = (
        [pl.BlockSpec(memory_space=memory[letter]) for letter in part] for part in specs.split(">")
    )
    return pl.pallas_call(
        kernel,
        name=name,
        out_shape=tuple(jax.ShapeDtypeStruct(shape, dtype) for shape, dtype in outs),
        in_specs=ins,
        out_specs=tuple(results),
        scratch_shapes=scratch,
        input_output_aliases=aliases or {},
        cost_estimate=pl.CostEstimate(flops=cost, bytes_accessed=0, transcendentals=0),
        compiler_params=pltpu.CompilerParams(vmem_limit_bytes=VMEM_LIMIT),
    )


def shards(features, cotangent, tile_mask, work_lists, dilations, conv_weight, conv_bias):
    x, cot, lists = features[0], cotangent[0], work_lists[0]
    rows, columns, channels = x.shape
    axes = ("tile", "dp")
    devices = lax.axis_size("tile") * lax.axis_size("dp")
    weight = conv_weight.reshape(9, channels, channels)
    bias = conv_bias.reshape(1, channels)
    inner = rows - 2 * HALO
    wide_row = 3 * channels
    pad = pltpu.VMEM((columns + 2 * EDGE, channels), F32)
    work = 2 * rows * columns * 9 * channels * channels

    low, high = exchange(x[rows - HALO :], x[:HALO], "tile")

    pre, grad, xt, total, mask, cot_edge = call(
        first_kernel,
        "first",
        [
            ((2 * HALO, columns, channels), F32),
            ((inner, columns, channels), BF16),
            ((rows, channels, columns), BF16),
            ((wide_row, wide_row), F32),
            ((3, columns, channels), BF16),
            ((2 * HALO, columns, channels), BF16),
        ],
        "svhhhv>vvvvvv",
        [
            pltpu.VMEM((rows, columns, channels), BF16),
            pltpu.VMEM((rows, columns, channels), BF16),
            pltpu.VMEM((9, channels, channels), BF16),
            pad,
            pltpu.VMEM((3, columns, channels), F32),
            pltpu.VMEM((rows + 2 * HALO, columns, wide_row), BF16),
            pltpu.VMEM((2 * columns, wide_row), BF16),
            pltpu.VMEM((4 * wide_row, 2 * channels), BF16),
            pltpu.VMEM((rows, columns, channels), F32),
            pltpu.SemaphoreType.DMA((5,)),
        ],
        2 * work,
    )(dilations, lists, x, cot, weight, bias)

    grad_low, grad_high, xt_halo = call(
        rims_kernel,
        "rims",
        [
            ((HALO, columns, channels), BF16),
            ((HALO, columns, channels), BF16),
            ((2 * HALO, channels, columns), BF16),
        ],
        "svvvvvv>vvv",
        [
            pad,
            pltpu.VMEM((HALO * columns, wide_row), BF16),
            pltpu.VMEM((2 * HALO, columns, channels), F32),
        ],
        work // 6,
    )(dilations, low, high, pre, cot_edge, mask, weight)

    from_low, from_high = exchange(grad_high, grad_low, "tile")

    tap_rows = 9 * channels
    direct = tap_rows % devices == 0
    share = (devices, tap_rows // devices) if direct else (1, tap_rows)
    (taps,) = call(
        taps_kernel,
        "taps",
        [(share + (channels,), BF16)],
        "svvvvv>v",
        [
            pad,
            pltpu.VMEM((HALO * columns, wide_row), BF16),
            pltpu.VMEM((6 * HALO, channels, columns), BF16),
            pltpu.VMEM((wide_row, wide_row), F32),
            pltpu.VMEM((tap_rows, channels), F32),
        ],
        work // 3,
    )(dilations, grad_low, grad_high, xt, xt_halo, total)
    if not direct:
        taps = taps.reshape(devices, -1)
    received = lax.all_to_all(taps, axes, 0, 0, tiled=True)

    held, edge = call(
        inputs_kernel,
        "inputs",
        [((rows, columns, channels), BF16), ((2 * HALO, columns, channels), F32)],
        "svvvhvv>hv",
        [
            pltpu.VMEM((rows, columns, channels), BF16),
            pltpu.VMEM((inner, columns, channels), BF16),
            pad,
            pltpu.VMEM((rows + 2 * HALO, columns, wide_row), BF16),
            pltpu.VMEM((2 * channels, 4 * wide_row), BF16),
            pltpu.VMEM((rows, columns, channels), F32),
            pltpu.SemaphoreType.DMA((2,)),
        ],
        2 * work,
    )(dilations, grad, grad_low, grad_high, cot, mask, weight)

    (input_grad,) = call(
        edges_kernel,
        "edges",
        [((rows, columns, channels), BF16)],
        "svvvvvh>h",
        [
            pltpu.VMEM((2 * HALO, columns, channels), BF16),
            pad,
            pltpu.VMEM((HALO * columns, wide_row), BF16),
            pltpu.VMEM((2 * HALO, columns, channels), F32),
            pltpu.SemaphoreType.DMA((2,)),
        ],
        work // 6,
        {6: 0},
    )(dilations, from_low, from_high, edge, mask, weight, held)

    grad_scale = 1.0 / math.sqrt(devices * lists.shape[1] * TILE * TILE)
    summed = jnp.sum(received.astype(F32), axis=0) * grad_scale
    return (input_grad[None], summed.reshape(-1))


def solution(mesh):
    placed = (
        P("dp", "tile", None, None),
        P("dp", "tile", None, None),
        P("dp", "tile", None),
        P("dp", None, None),
        P("dp", None),
        P(),
        P(),
    )
    return jax.shard_map(
        shards,
        mesh=mesh,
        in_specs=placed,
        out_specs=(P("dp", "tile", None, None), P(("tile", "dp"))),
        check_vma=False,
    )
```

time: 62.4 us -> 53.4 us (0.86)
  waiting for transfers between devices: 15 us -> 5.1 us
  starting transfers between devices: 16.6 us -> 18.9 us
  other arithmetic: 1.89 us -> 0.67 us
    ppermute x2, waiting for transfers between devices: 8.48 us -> 3.06 us  [exchange(): lax.ppermute(to_next, axis, forward)]
    ppermute x2, waiting for transfers between devices: 6.51 us -> 2.04 us  [exchange(): lax.ppermute(to_previous, axis, backward)]
    all_to_all x1, starting transfers between devices: 4.93 us -> 7.14 us  [shards(): received = lax.all_to_all(taps, axes, 0, 0, tiled=True)]
    unnamed x14 -> x18, local copies, waits for them, and re-layouts: 4.17 us -> 5.52 us
    reduce_or x1 -> x0, other arithmetic: 1.09 us -> none  [shards(): observed = jnp.any(ids[:, None, None] == targets[None], axis=0).astype(F32)]
    eq x1 -> x0, local copies, waits for them, and re-layouts: 0.78 us -> none  [shards(): observed = jnp.any(ids[:, None, None] == targets[None], axis=0).astype(F32)]
    pallas_call x3 -> x5, Pallas kernels: 21.1 us -> 21 us  [the longest x1 9.29 us: shards(): call(first_kernel, 'first', [((2 * HALO, columns, channels), F32), ((inne...]
  transfers between devices with their start and end apart: 5 -> 5, of which waited for: 4 -> 2; matrix products, arithmetic and copies ran while one was open for 4% -> 0% of each run, Pallas kernels for 13% -> 32%
where the time goes in v1:
time: 53.4 us; the launch traced here: 53 us
  Pallas kernels  21 us (39%)
  starting transfers between devices  18.9 us (35%)
  local copies, waits for them, and re-layouts  6.57 us (12%)
  waiting for transfers between devices  5.1 us (10%)
  between operations  0.78 us (1%)
  other arithmetic  0.67 us (1%)
    pallas_call x1, Pallas kernels, shards(): call(first_kernel, 'first', [((2 * HALO, columns, channels), F32), ((inne...  9.29 us
    ppermute x2, starting transfers between devices, exchange(): lax.ppermute(to_next, axis, forward)  9.17 us
    all_to_all x1, starting transfers between devices, shards(): received = lax.all_to_all(taps, axes, 0, 0, tiled=True)  7.14 us
    pallas_call x1, Pallas kernels, shards(): call(inputs_kernel, 'inputs', [((rows, columns, channels), BF16), ((2 * H...  5.87 us
    unnamed x18, local copies, waits for them, and re-layouts  5.52 us
    ppermute x2, waiting for transfers between devices, exchange(): lax.ppermute(to_next, axis, forward)  3.06 us
    ppermute x2, starting transfers between devices, exchange(): lax.ppermute(to_previous, axis, backward)  2.58 us
    pallas_call x1, Pallas kernels, shards(): call(taps_kernel, 'taps', [(share + (channels,), BF16)], 'svvvvv>v', [pad...  2.39 us
  transfers between devices with their start and end apart: 5, of which 2 were waited for; matrix products, arithmetic and copies ran while one was open for 0% of the time, Pallas kernels for 32%

profile of v1, /device:TPU:0, one launch (start us, length us, event | category | flops | bytes accessed | tf_op | source)
XLA Modules:
  0.0 53.0 jit_solution(17683426682302993)
XLA Ops:
  0.6 1.1 %slice_bitcast_fusion = (bf16[2,384,128]{2,1,0:T(8,128)(2,1)S(1)}, bf16[2,384,128]{2,1,0:T(8,128)(2,1)S(1)}) fusion(bf16[1,12,384,128]{3,2,1,0:T(8,128)(2,1)} %param.7), kind=kLoop, calls=%fused_computation.1 | loop fusion | bytes 786432 | tf_op jit(solution)/shard_map/slice | solution.py:358
  1.7 1.3 %collective-permute-start.1 = (bf16[2,384,128]{2,1,0:T(8,128)(2,1)S(1)}, bf16[2,384,128]{2,1,0:T(8,128)(2,1)S(1)}, u32[]{:S(2)}, u32[]{:S(2)}) collective-permute-start(bf16[2,384,128]{2,1,0:T(8,128)(2,1)S(1)} %get-tuple-element.24), channel_id=1, source_target_pairs={{2,0},{4,2},{6,4},{8,6},{10,8},{12,10},{14,12},{16,14},{18,16},{20... | collective-permute-start | bytes 589832 | tf_op jit(solution)/shard_map/ppermute | solution.py:325
  3.0 5.5 %collective-permute-start = (bf16[2,384,128]{2,1,0:T(8,128)(2,1)S(1)}, bf16[2,384,128]{2,1,0:T(8,128)(2,1)S(1)}, u32[]{:S(2)}, u32[]{:S(2)}) collective-permute-start(bf16[2,384,128]{2,1,0:T(8,128)(2,1)S(1)} %get-tuple-element.25), channel_id=1, source_target_pairs={{0,2},{2,4},{4,6},{6,8},{8,10},{10,12},{12,14},{14,16},{16,18},{18... | collective-permute-start | bytes 589832 | tf_op jit(solution)/shard_map/ppermute | solution.py:325
  8.5 0.0 copy-start
  8.5 1.0 %copy-done = bf16[3,3,128,128]{3,2,1,0:T(8,128)(2,1)S(1)} copy-done((bf16[3,3,128,128]{3,2,1,0:T(8,128)(2,1)S(1)}, bf16[3,3,128,128]{3,2,1,0:T(8,128)(2,1)}, u32[]{:S(2)}) %copy-start) | copy-done | bytes 294936
  9.4 1.3 %copy-done.2 = bf16[1,12,384,128]{3,2,1,0:T(8,128)(2,1)S(1)} copy-done((bf16[1,12,384,128]{3,2,1,0:T(8,128)(2,1)S(1)}, bf16[1,12,384,128]{3,2,1,0:T(8,128)(2,1)}, u32[]{:S(2)}) %copy-start.2) | copy-done | bytes 1179672
  10.7 0.0 copy-start.3
  10.7 0.7 %copy-done.3 = s32[1,16]{1,0:T(1,128)S(1)} copy-done((s32[1,16]{1,0:T(1,128)S(1)}, s32[1,16]{1,0:T(1,128)}, u32[]{:S(2)}) %copy-start.3) | copy-done | bytes 88
  11.4 0.0 copy-start.5
  11.4 1.3 %copy-done.5 = bf16[1,12,384,128]{3,2,1,0:T(8,128)(2,1)S(1)} copy-done((bf16[1,12,384,128]{3,2,1,0:T(8,128)(2,1)S(1)}, bf16[1,12,384,128]{3,2,1,0:T(8,128)(2,1)}, u32[]{:S(2)}) %copy-start.5) | copy-done | bytes 1179672
  12.6 0.7 %copy-done.7 = s32[1,16,22]{2,1,0:T(8,128)S(1)} copy-done((s32[1,16,22]{2,1,0:T(8,128)S(1)}, s32[1,16,22]{2,1,0:T(8,128)}, u32[]{:S(2)}) %copy-start.7) | copy-done | bytes 1432
  13.3 0.7 %copy-done.8 = f32[128]{0:T(128)S(1)} copy-done((f32[128]{0:T(128)S(1)}, f32[128]{0:T(128)}, u32[]{:S(2)}) %copy-start.8) | copy-done | bytes 536
  14.0 9.3 %first.1 = (f32[4,384,128]{2,1,0:T(8,128)S(1)}, bf16[8,384,128]{2,1,0:T(8,128)(2,1)S(1)}, bf16[12,128,384]{2,1,0:T(8,128)(2,1)S(1)}, f32[384,384]{1,0:T(8,128)S(...) custom-call(s32[1,16]{1,0:T(1,128)S(1)} %copy-done.3, s32[16,22]{1,0:T(8,128)S(1)} %bitcast.19, ...), custom_call_target="tpu_custom_call" | custom-call | flops 2717908992 | tf_op jit(solution)/shard_map/first/pallas_call | solution.py:360
  23.3 0.0 collective-permute-done.1.high_ref
  23.3 0.0 collective-permute-done.low_ref
  23.3 0.0 copy-done.1
  23.3 1.5 %rims.1 = (bf16[2,384,128]{2,1,0:T(8,128)(2,1)S(1)}, bf16[2,384,128]{2,1,0:T(8,128)(2,1)S(1)}, bf16[4,128,384]{2,1,0:T(8,128)(2,1)S(1)}) custom-call(s32[1,16]{1,0:T(1,128)S(1)} %copy-done.3, bf16[2,384,128]{2,1,0:T(8,128)(2,1)S(1)} %collective-permute-done.low_ref, bf16[2,384,128]{2,1,0:T(8,128)(2,1)S(1)} %collective-permute-done.1.high_ref, ...), custom_call_target="tpu_custom_call" | custom-call | flops 226492416 | tf_op jit(solution)/shard_map/rims/pallas_call | solution.py:387
  24.8 0.0 copy-start.4
  24.8 0.0 copy-start.6
  24.8 2.4 %taps.1 = bf16[32,36,128]{2,1,0:T(8,128)(2,1)} custom-call(s32[1,16]{1,0:T(1,128)S(1)} %copy-done.3, bf16[2,384,128]{2,1,0:T(8,128)(2,1)S(1)} %get-tuple-element.17.grad_low_ref, bf16[2,384,128]{2,1,0:T(8,128)(2,1)S(1)} %get-tuple-element.16.grad_high_ref, bf16[12,128,384]{2,1,0:T(8,128)(2,1)S(1)} %get-tuple-element.21.xt_own_ref, ...), custom_call_target="tpu_custom_call" | custom-call | flops 452984832 | tf_op jit(solution)/shard_map/taps/pallas_call | solution.py:409
  27.2 7.1 %all-to-all-start = ((bf16[32,36,128]{2,1,0:T(8,128)(2,1)}), bf16[32,36,128]{2,1,0:T(8,128)(2,1)S(1)}, u32[]{:S(2)}, u32[]{:S(2)}) async-start(bf16[32,36,128]{2,1,0:T(8,128)(2,1)} %taps.1), calls=%async_computation | async-start | bytes 655360 | tf_op jit(solution)/shard_map/all_to_all | solution.py:425
  34.4 3.7 %collective-permute-start.2 = (bf16[2,384,128]{2,1,0:T(8,128)(2,1)S(1)}, bf16[2,384,128]{2,1,0:T(8,128)(2,1)S(1)}, u32[]{:S(2)}, u32[]{:S(2)}) collective-permute-start(bf16[2,384,128]{2,1,0:T(8,128)(2,1)S(1)} %get-tuple-element.16.grad_high_ref), channel_id=1, source_target_pairs={{0,2},{2,4},{4,6},{6,8},{8,10},{10,12},{12,14},{14,16},{16,18},{18... | collective-permute-start | bytes 589832 | tf_op jit(solution)/shard_map/ppermute | solution.py:325
  38.1 1.3 %collective-permute-start.3 = (bf16[2,384,128]{2,1,0:T(8,128)(2,1)S(1)}, bf16[2,384,128]{2,1,0:T(8,128)(2,1)S(1)}, u32[]{:S(2)}, u32[]{:S(2)}) collective-permute-start(bf16[2,384,128]{2,1,0:T(8,128)(2,1)S(1)} %get-tuple-element.17.grad_low_ref), channel_id=1, source_target_pairs={{2,0},{4,2},{6,4},{8,6},{10,8},{12,10},{14,12},{16,14},{18,16},{20... | collective-permute-start | bytes 589832 | tf_op jit(solution)/shard_map/ppermute | solution.py:325
  39.4 0.0 copy-done.4
  39.4 0.0 copy-done.6
  39.4 5.9 %inputs.1 = (bf16[12,384,128]{2,1,0:T(8,128)(2,1)}, f32[4,384,128]{2,1,0:T(8,128)S(1)}) custom-call(s32[1,16]{1,0:T(1,128)S(1)} %copy-done.4, bf16[8,384,128]{2,1,0:T(8,128)(2,1)S(1)} %get-tuple-element.18.grad_ref, bf16[2,384,128]{2,1,0:T(8,128)(2,1)S(1)} %get-tuple-element.17.grad_low_ref, bf16[2,384,128]{2,1,0:T(8,128)(2,1)S(1)} %get-tuple-element.16.grad_high_ref, ...), custom_call_target="tpu_custom_call" | custom-call | flops 2717908992 | tf_op jit(solution)/shard_map/inputs/pallas_call | solution.py:427
  45.3 3.1 %collective-permute-done.2.low_ref = bf16[2,384,128]{2,1,0:T(8,128)(2,1)S(1)} collective-permute-done((bf16[2,384,128]{2,1,0:T(8,128)(2,1)S(1)}, bf16[2,384,128]{2,1,0:T(8,128)(2,1)S(1)}, u32[]{:S(2)}, u32[]{:S(2)}) %collective-permute-start.2) | collective-permute-done | bytes 196640 | tf_op jit(solution)/shard_map/ppermute | solution.py:325
  48.3 2.0 %collective-permute-done.3.high_ref = bf16[2,384,128]{2,1,0:T(8,128)(2,1)S(1)} collective-permute-done((bf16[2,384,128]{2,1,0:T(8,128)(2,1)S(1)}, bf16[2,384,128]{2,1,0:T(8,128)(2,1)S(1)}, u32[]{:S(2)}, u32[]{:S(2)}) %collective-permute-start.3) | collective-permute-done | bytes 196640 | tf_op jit(solution)/shard_map/ppermute | solution.py:325
  50.3 2.0 %edges.1 = bf16[12,384,128]{2,1,0:T(8,128)(2,1)} custom-call(s32[1,16]{1,0:T(1,128)S(1)} %copy-done.4, bf16[2,384,128]{2,1,0:T(8,128)(2,1)S(1)} %collective-permute-done.2.low_ref, bf16[2,384,128]{2,1,0:T(8,128)(2,1)S(1)} %collective-permute-done.3.high_ref, f32[4,384,128]{2,1,0:T(8,128)S(1)} %get-tuple-element.19.edge_ref, ...), custom_call_target="tpu_custom_call", output_to_operand_aliasing={{}: (6, {})} | custom-call | flops 226492416 | tf_op jit(solution)/shard_map/edges/pallas_call | solution.py:444
  52.3 0.0 all-to-all-done
  52.3 0.1 convert_reduce_fusion
  52.4 0.6 %multiply_bitcast_fusion = f32[4608]{0:T(1024)} fusion(f32[36,128]{1,0:T(8,128)S(1)} %convert_reduce_fusion), kind=kLoop, calls=%fused_computation.3 | loop fusion | flops 4608 | bytes 36864 | tf_op jit(solution)/shard_map/mul | solution.py:461
  (4 shorter events, 0.0 us)
Async XLA Ops:
  1.7 21.6 %collective-permute-start.1 = (bf16[2,384,128]{2,1,0:T(8,128)(2,1)S(1)}, bf16[2,384,128]{2,1,0:T(8,128)(2,1)S(1)}, u32[]{:S(2)}, u32[]{:S(2)}) collective-permute-start(bf16[2,384,128]{2,1,0:T(8,128)(2,1)S(1)} %get-tuple-element.24), channel_id=1, source_target_pairs={{2,0},{4,2},{6,4},{8,6},{10,8},{12,10},{14,12},{16,14},{18,16},{20... | collective-permute-start | bytes 589832 | tf_op jit(solution)/shard_map/ppermute | solution.py:325
  3.0 20.3 %collective-permute-start = (bf16[2,384,128]{2,1,0:T(8,128)(2,1)S(1)}, bf16[2,384,128]{2,1,0:T(8,128)(2,1)S(1)}, u32[]{:S(2)}, u32[]{:S(2)}) collective-permute-start(bf16[2,384,128]{2,1,0:T(8,128)(2,1)S(1)} %get-tuple-element.25), channel_id=1, source_target_pairs={{0,2},{2,4},{4,6},{6,8},{8,10},{10,12},{12,14},{14,16},{16,18},{18... | collective-permute-start | bytes 589832 | tf_op jit(solution)/shard_map/ppermute | solution.py:325
  8.5 1.0 %copy-start = (bf16[3,3,128,128]{3,2,1,0:T(8,128)(2,1)S(1)}, bf16[3,3,128,128]{3,2,1,0:T(8,128)(2,1)}, u32[]{:S(2)}) copy-start(bf16[3,3,128,128]{3,2,1,0:T(8,128)(2,1)} %param.11) | copy-start | bytes 884740
  9.4 1.3 %copy-start.2 = (bf16[1,12,384,128]{3,2,1,0:T(8,128)(2,1)S(1)}, bf16[1,12,384,128]{3,2,1,0:T(8,128)(2,1)}, u32[]{:S(2)}) copy-start(bf16[1,12,384,128]{3,2,1,0:T(8,128)(2,1)} %param.7) | copy-start | bytes 3538948
  10.7 0.7 %copy-start.3 = (s32[1,16]{1,0:T(1,128)S(1)}, s32[1,16]{1,0:T(1,128)}, u32[]{:S(2)}) copy-start(s32[1,16]{1,0:T(1,128)} %rates_ref.9) | copy-start | bytes 196
  11.4 1.3 %copy-start.5 = (bf16[1,12,384,128]{3,2,1,0:T(8,128)(2,1)S(1)}, bf16[1,12,384,128]{3,2,1,0:T(8,128)(2,1)}, u32[]{:S(2)}) copy-start(bf16[1,12,384,128]{3,2,1,0:T(8,128)(2,1)} %param.8) | copy-start | bytes 3538948
  12.6 0.7 %copy-start.7 = (s32[1,16,22]{2,1,0:T(8,128)S(1)}, s32[1,16,22]{2,1,0:T(8,128)}, u32[]{:S(2)}) copy-start(s32[1,16,22]{2,1,0:T(8,128)} %param.9) | copy-start | bytes 4228
  13.3 0.7 %copy-start.8 = (f32[128]{0:T(128)S(1)}, f32[128]{0:T(128)}, u32[]{:S(2)}) copy-start(f32[128]{0:T(128)} %param.12) | copy-start | bytes 1540
  14.0 9.3 %copy-start.1 = (bf16[3,3,128,128]{3,2,1,0:T(8,128)(2,1)S(1)}, bf16[3,3,128,128]{3,2,1,0:T(8,128)(2,1)}, u32[]{:S(2)}) copy-start(bf16[3,3,128,128]{3,2,1,0:T(8,128)(2,1)} %param.11) | copy-start | bytes 884740
  24.8 14.6 %copy-start.4 = (s32[1,16]{1,0:T(1,128)S(1)}, s32[1,16]{1,0:T(1,128)}, u32[]{:S(2)}) copy-start(s32[1,16]{1,0:T(1,128)} %rates_ref.9) | copy-start | bytes 196
  24.8 14.6 %copy-start.6 = (bf16[1,12,384,128]{3,2,1,0:T(8,128)(2,1)S(1)}, bf16[1,12,384,128]{3,2,1,0:T(8,128)(2,1)}, u32[]{:S(2)}) copy-start(bf16[1,12,384,128]{3,2,1,0:T(8,128)(2,1)} %param.8) | copy-start | bytes 3538948
  27.2 25.1 %all-to-all-start = ((bf16[32,36,128]{2,1,0:T(8,128)(2,1)}), bf16[32,36,128]{2,1,0:T(8,128)(2,1)S(1)}, u32[]{:S(2)}, u32[]{:S(2)}) async-start(bf16[32,36,128]{2,1,0:T(8,128)(2,1)} %taps.1), calls=%async_computation | async-start | bytes 655360 | tf_op jit(solution)/shard_map/all_to_all | solution.py:425
  34.4 13.9 %collective-permute-start.2 = (bf16[2,384,128]{2,1,0:T(8,128)(2,1)S(1)}, bf16[2,384,128]{2,1,0:T(8,128)(2,1)S(1)}, u32[]{:S(2)}, u32[]{:S(2)}) collective-permute-start(bf16[2,384,128]{2,1,0:T(8,128)(2,1)S(1)} %get-tuple-element.16.grad_high_ref), channel_id=1, source_target_pairs={{0,2},{2,4},{4,6},{6,8},{8,10},{10,12},{12,14},{14,16},{16,18},{18... | collective-permute-start | bytes 589832 | tf_op jit(solution)/shard_map/ppermute | solution.py:325
  38.1 12.3 %collective-permute-start.3 = (bf16[2,384,128]{2,1,0:T(8,128)(2,1)S(1)}, bf16[2,384,128]{2,1,0:T(8,128)(2,1)S(1)}, u32[]{:S(2)}, u32[]{:S(2)}) collective-permute-start(bf16[2,384,128]{2,1,0:T(8,128)(2,1)S(1)} %get-tuple-element.17.grad_low_ref), channel_id=1, source_target_pairs={{2,0},{4,2},{6,4},{8,6},{10,8},{12,10},{14,12},{16,14},{18,16},{20... | collective-permute-start | bytes 589832 | tf_op jit(solution)/shard_map/ppermute | solution.py:325
